TPU v7x, 32 devices: a whole 2x2x4 slice. The times are simulated.
32 devices in a mesh: seq: 4 (over y, x), dp: 8 (over z, core).
Axes of the slice: x: 2, y: 2, z: 4, core: 2. Of those that a mesh axis runs over, the one named last changes fastest.
Arguments:
- queries: bfloat16 [8, 1024, 1024], P('dp', 'seq'), may hold values from -1.75 to 1.75
- keys: bfloat16 [8, 1024, 1024], P('dp', 'seq'), may hold values from -1.75 to 1.75
- values: bfloat16 [8, 1024, 1024], P('dp', 'seq'), may hold values from -6 to 6
- out_grad: bfloat16 [8, 1024, 1024], P('dp', 'seq'), may hold values from -6 to 6
- out_weight: bfloat16 [1024, 1024], P('dp'), may hold values from -0.1875 to 0.1875
- block_mask: int32 [8, 32, 8], P('dp', 'seq'), may hold values 0 or 1
Outputs:
- layer_out: bfloat16 [8, 1024, 1024], P('dp', 'seq')
- query_grad: bfloat16 [8, 1024, 1024], P('dp', 'seq')
- key_grad: bfloat16 [8, 1024, 1024], P('dp', 'seq')
- value_grad: bfloat16 [8, 1024, 1024], P('dp', 'seq')
- weight_grad: float32 [1024, 1024], P('dp')
Inputs may be any that keep to these rules, and one draw needn't show every extreme that they name: `block_mask`: entries for key blocks at or after the query's own block are not read.
All inputs are finite; a program needn't handle non-finite values.
Results may differ from a plain program's by a relative error of at most 0.017.
Values may be sent and summed in bfloat16 or wider, within the bound.
A program may use at most 128 MiB of HBM per device.

v0:
```python
import functools
import math

import jax
import jax.numpy as jnp
from jax import lax
from jax.experimental import pallas as pl
from jax.experimental.pallas import tpu as pltpu
from jax.sharding import PartitionSpec as P

H = 8
norm_eps = 1e-05
MESH = pl.DeviceIdType.MESH
f32 = jnp.float32
bf16 = jnp.bfloat16
QUAD = 4
CHUNKS = 4
UNROLL = 4


def bit(i, m):
    return lax.rem(lax.div(i, m), 2)


def flip(i, m):
    return i + m - 2 * m * bit(i, m)


def mm(a, b, da, db):
    return lax.dot_general(a, b, (((da,), (db,)), ((), ())), preferred_element_type=f32)


def over_heads(lo, hi, fn):
    if hi <= lo:
        return

    def body(h, c):
        fn(h)
        return c

    lax.fori_loop(lo, hi, body, 0, unroll=UNROLL)


def visibility(mask, tokens):
    blocks = mask.shape[0]
    width = tokens // blocks
    t = lax.broadcasted_iota(jnp.int32, (tokens, blocks), 0)
    b = lax.broadcasted_iota(jnp.int32, (tokens, blocks), 1) * width
    member = jnp.where((t >= b) & (t < b + width), 1.0, 0.0)
    r = lax.broadcasted_iota(jnp.int32, (blocks, blocks), 0)
    c = lax.broadcasted_iota(jnp.int32, (blocks, blocks), 1)
    lower = jnp.where((mask == 1) & (c < r), 1.0, 0.0)
    member = member.astype(bf16)
    rows = mm(member, lower.astype(bf16), 1, 0).astype(bf16)
    earlier = mm(rows, member, 1, 1)
    same = mm(member, member, 1, 1)
    row = lax.broadcasted_iota(jnp.int32, (tokens, tokens), 0)
    col = lax.broadcasted_iota(jnp.int32, (tokens, tokens), 1)
    return earlier + jnp.where(col <= row, same, 0.0)


def kernel(
    n_seq, n_dp, q_hbm, k_hbm, v_hbm, g_hbm, w_ref, mask_hbm,
    out_ref, qg_ref, kg_ref, vg_ref, wg_ref,
    w_full, vis_ref, s_out, s_in, acc, prior, later, wts, attn, inv, normed,
    dnormed, dattn, dsc, term, a_in, u_out, x_in, z_out, z_in, z_own, r_out, r_in, f_out,
    w1_s, w1_r, w2_s, w2_r, w3_s, w3_r, st_s, st_r, a_s, a_r, x_s, x_r, z_s, z_r, r_s, r_r,
    f_s, f_r, q_ref, k_ref, v_ref, g_ref, mask_ref, in_s,
):
    tokens, width = q_ref.shape
    size = width // H
    n_z = n_dp // 2
    rows = w_ref.shape[0]
    cols = w_ref.shape[1]
    quarter = cols // QUAD
    n_bits = n_seq.bit_length() - 1
    s = lax.axis_index("seq")
    d = lax.axis_index("dp")
    z = lax.div(d, 2)
    core = lax.rem(d, 2)
    s4 = lax.rem(s, QUAD)
    peer = flip(d, 1)
    seq_peer = {j: s for j in (1, 2, 3)}
    seq_peer[1] = flip(s, 1)
    seq_peer[2] = flip(s, 2)
    seq_peer[3] = flip(flip(s, 1), 2)

    def qcols(seq_index):
        return pl.ds(pl.multiple_of(lax.rem(seq_index, QUAD) * quarter, quarter), quarter)

    def brow(dp_index):
        return pl.ds(pl.multiple_of(dp_index * rows, rows), rows)

    def hcols(h):
        return pl.ds(pl.multiple_of(h * size, size), size)

    def up(k):
        return lax.rem(z + k, n_z)

    def down(k):
        return lax.rem(z + n_z - k, n_z)

    def rc(src, dst, ss, rs, dev):
        return pltpu.make_async_remote_copy(
            src_ref=src, dst_ref=dst, send_sem=ss, recv_sem=rs, device_id=dev,
            device_id_type=MESH,
        )

    sent = []

    def go(*a):
        c = rc(*a)
        c.start()
        sent.append(c)

    def arrive(dst, ss, rs, dev):
        rc(dst, dst, ss, rs, dev).wait_recv()

    loads = {}
    pairs = [(k_hbm, k_ref), (v_hbm, v_ref), (q_hbm, q_ref), (mask_hbm, mask_ref), (g_hbm, g_ref)]
    pairs.append((w_ref, w_full.at[brow(d)]))
    for i, name in enumerate("kvqmgw"):
        loads[name] = pltpu.make_async_copy(pairs[i][0], pairs[i][1], in_s.at[i])
        loads[name].start()

    barrier = pltpu.get_barrier_semaphore()
    partners = [(s, peer)]
    partners += [(seq_peer[j], d) for j in (1, 2, 3)]
    partners += [(flip(s, 1 << b), d) for b in range(2, n_bits)]
    partners += [(s, up(i) * 2 + core) for i in range(1, n_z)]
    for p in partners:
        pl.semaphore_signal(barrier, inc=1, device_id=p, device_id_type=MESH)
    pl.semaphore_wait(barrier, len(partners))

    own_q = [qcols(s), qcols(seq_peer[3])]
    for part in range(2):
        for i in range(1, n_z):
            go(
                w_ref.at[:, own_q[part]], w_full.at[brow(d), own_q[part]],
                w1_s.at[part, i - 1], w1_r.at[part, i - 1], (s, up(i) * 2 + core),
            )
    go(w_ref, w_full.at[brow(d)], w3_s.at[0], w3_r.at[0], (s, peer))
    loads["k"].wait()
    loads["v"].wait()

    half = width // CHUNKS

    def chunk(c):
        return pl.ds(c * half, half)

    def send_state(way, b, c):
        go(
            s_out.at[way, b, chunk(c)], s_in.at[way, b, chunk(c)],
            st_s.at[way, b, c], st_r.at[way, b, c], (flip(s, 1 << b), d),
        )

    def state_step(way, b, c):
        arrive(s_in.at[way, b, chunk(c)], st_s.at[way, b, c], st_r.at[way, b, c], (flip(s, 1 << b), d))
        got = s_in[way, b, chunk(c)].astype(f32)
        if b + 1 < n_bits:
            s_out[way, b + 1, chunk(c)] = (s_out[way, b, chunk(c)].astype(f32) + got).astype(bf16)
            send_state(way, b + 1, c)
        own_bit = bit(s, 1 << b)
        use = (own_bit if way == 0 else 1 - own_bit).astype(f32)
        if b == 0:
            acc[chunk(c)] = got * use
        else:
            acc[chunk(c)] += got * use

    per = H // CHUNKS
    for c in range(CHUNKS):

        def make_state(h):
            st = mm(k_ref[:, hcols(h)], v_ref[:, hcols(h)], 0, 0)
            s_out[0, 0, hcols(h)] = st.astype(bf16)

        over_heads(c * per, (c + 1) * per, make_state)
        send_state(0, 0, c)

    loads["q"].wait()
    loads["m"].wait()
    vis_ref[...] = visibility(mask_ref[...], tokens)

    def local_attn(h):
        sc = mm(q_ref[:, hcols(h)], k_ref[:, hcols(h)], 1, 1)
        wt = (sc * vis_ref[...]).astype(bf16)
        wts[h] = wt
        attn[:, hcols(h)] = mm(wt, v_ref[:, hcols(h)], 1, 0)

    over_heads(0, H, local_attn)

    for c in range(CHUNKS):
        state_step(0, 0, c)

    for i in range(1, n_z):
        src = down(i) * 2 + core
        arrive(w_full.at[brow(src), own_q[0]], w1_s.at[0, i - 1], w1_r.at[0, i - 1], (s, src))
        for j in (1, 2):
            go(
                w_full.at[brow(src), own_q[0]], w_full.at[brow(src), own_q[0]],
                w2_s.at[j - 1, i - 1], w2_r.at[j - 1, i - 1], (seq_peer[j], d),
            )

    for b in range(1, n_bits):
        for c in range(CHUNKS):
            state_step(0, b, c)
    prior[...] = acc[...].astype(bf16)

    loads["g"].wait()
    loads["w"].wait()

    def finish_attn(h):
        a = attn[:, hcols(h)] + mm(q_ref[:, hcols(h)], prior[hcols(h), :], 1, 0)
        iv = lax.rsqrt(jnp.mean(a * a, -1, keepdims=True) + norm_eps)
        u = a * iv
        attn[:, hcols(h)] = u
        inv[h] = iv
        n = u.astype(bf16)
        normed[:, hcols(h)] = n
        term[hcols(h), :] = mm(n, g_ref[...], 0, 0).astype(bf16)

    over_heads(0, H, finish_attn)

    for i in range(n_z):
        zz = up(i + 1)
        go(
            term.at[brow(zz * 2 + 1 - core)], a_in.at[zz], a_s.at[i], a_r.at[i], (s, peer)
        )

    for i in range(1, n_z):
        src = down(i) * 2 + core
        arrive(w_full.at[brow(src), own_q[1]], w1_s.at[1, i - 1], w1_r.at[1, i - 1], (s, src))
        for j in (1, 2):
            arrive(
                w_full.at[brow(src), qcols(seq_peer[j])], w2_s.at[j - 1, i - 1],
                w2_r.at[j - 1, i - 1], (seq_peer[j], d),
            )
        go(w_full.at[brow(src)], w_full.at[brow(src)], w3_s.at[i], w3_r.at[i], (s, peer))

    for i in range(n_z):
        zz = up(i + 1)
        arrive(a_in.at[zz], a_s.at[i], a_r.at[i], (s, peer))
        u_out[zz] = (term[brow(zz * 2 + core), :].astype(f32) + a_in[zz].astype(f32)).astype(bf16)
        for j in (1, 2, 3):
            go(
                u_out.at[zz, :, qcols(seq_peer[j])], x_in.at[j - 1, zz],
                x_s.at[j - 1, i], x_r.at[j - 1, i], (seq_peer[j], d),
            )

    for i in range(n_z):
        src = down(i) * 2 + 1 - core
        arrive(w_full.at[brow(src)], w3_s.at[i], w3_r.at[i], (s, peer))

    def grad_norm(h):
        dn = mm(g_ref[...], w_full[hcols(h), :], 1, 1)
        u = attn[:, hcols(h)]
        da = (inv[h] * (dn - u * jnp.mean(dn * u, -1, keepdims=True))).astype(bf16)
        dattn[:, hcols(h)] = da
        s_out[1, 0, hcols(h)] = mm(q_ref[:, hcols(h)], da, 0, 0).astype(bf16)

    for c in range(CHUNKS):
        over_heads(c * per, (c + 1) * per, grad_norm)
        send_state(1, 0, c)

    def z_step(i):
        zz = up(i + 1)
        total = u_out[zz, :, qcols(s)].astype(f32)
        for j in (1, 2, 3):
            arrive(x_in.at[j - 1, zz], x_s.at[j - 1, i], x_r.at[j - 1, i], (seq_peer[j], d))
            total = total + x_in[j - 1, zz].astype(f32)
        if i < n_z - 1:
            z_out[i] = total.astype(bf16)
            go(z_out.at[i], z_in.at[i], z_s.at[i], z_r.at[i], (s, zz * 2 + core))
        else:
            z_own[...] = total

    def make_scores(h):
        ds = (mm(dattn[:, hcols(h)], v_ref[:, hcols(h)], 1, 1) * vis_ref[...]).astype(bf16)
        dsc[h] = ds
        qg = mm(ds, k_ref[:, hcols(h)], 1, 0) + mm(dattn[:, hcols(h)], prior[hcols(h), :], 1, 1)
        qg_ref[:, hcols(h)] = qg.astype(bf16)
        out_ref[:, hcols(h)] = mm(normed[...], w_full[:, hcols(h)], 1, 0).astype(bf16)

    for i in range(n_z):
        over_heads(i * H // n_z, (i + 1) * H // n_z, make_scores)
        z_step(i)

    for c in range(CHUNKS):
        state_step(1, 0, c)

    def local_grads(h):
        attn[:, hcols(h)] = mm(dsc[h], q_ref[:, hcols(h)], 0, 0)
        dnormed[:, hcols(h)] = mm(wts[h], dattn[:, hcols(h)], 0, 0)

    over_heads(0, H, local_grads)

    total = z_own[...]
    for i in range(n_z - 1):
        src = down(i + 1) * 2 + core
        arrive(z_in.at[i], z_s.at[i], z_r.at[i], (s, src))
        total = total + z_in[i].astype(f32)
    for b in range(2, n_bits):
        r_out[b - 2] = total.astype(bf16)
        dev = (flip(s, 1 << b), d)
        go(r_out.at[b - 2], r_in.at[b - 2], r_s.at[b - 2], r_r.at[b - 2], dev)
        arrive(r_in.at[b - 2], r_s.at[b - 2], r_r.at[b - 2], dev)
        total = total + r_in[b - 2].astype(f32)
    f_out[:, qcols(s)] = total.astype(bf16)
    for j in (1, 2, 3):
        go(
            f_out.at[:, qcols(s)], f_out.at[:, qcols(s)], f_s.at[j - 1], f_r.at[j - 1],
            (seq_peer[j], d),
        )

    for b in range(1, n_bits):
        for c in range(CHUNKS):
            state_step(1, b, c)
    later[...] = acc[...].astype(bf16)

    def last_grads(h):
        kg = attn[:, hcols(h)] + mm(v_ref[:, hcols(h)], later[hcols(h), :], 1, 1)
        kg_ref[:, hcols(h)] = kg.astype(bf16)
        vg = dnormed[:, hcols(h)] + mm(k_ref[:, hcols(h)], later[hcols(h), :], 1, 0)
        vg_ref[:, hcols(h)] = vg.astype(bf16)

    over_heads(0, H, last_grads)

    for j in (1, 2, 3):
        arrive(f_out.at[:, qcols(seq_peer[j])], f_s.at[j - 1], f_r.at[j - 1], (seq_peer[j], d))
    wg_ref[...] = f_out[...].astype(f32) * (1.0 / math.sqrt(n_seq * n_dp * tokens))
    for c in sent:
        c.wait_send()


def store(*refs):
    src, dst, buf, (load_s, save_s) = refs[:5], refs[5:10], refs[10:15], refs[15:]
    loads = [pltpu.make_async_copy(src[i], buf[i], load_s.at[i]) for i in range(5)]
    saves = [pltpu.make_async_copy(buf[i], dst[i], save_s.at[i]) for i in range(5)]
    for c in loads:
        c.start()
    for i in range(5):
        loads[i].wait()
        saves[i].start()
    for c in saves:
        c.wait()


def on_device(n_seq, n_dp, queries, keys, values, out_grad, out_weight, block_mask):
    _, tokens, width = queries.shape
    rows, cols = out_weight.shape
    size = width // H
    n_z = n_dp // 2
    n_bits = n_seq.bit_length() - 1
    more = max(n_bits - 2, 1)
    quarter = cols // QUAD
    dma = pltpu.SemaphoreType.DMA
    vm = pltpu.VMEM
    act = jax.ShapeDtypeStruct((tokens, width), bf16)
    spec = pl.BlockSpec(memory_space=pltpu.VMEM)
    outs = pl.pallas_call(
        functools.partial(kernel, n_seq, n_dp),
        out_shape=[act, act, act, act, jax.ShapeDtypeStruct((rows, cols), f32)],
        in_specs=[pl.BlockSpec(memory_space=pltpu.HBM)] * 6,
        out_specs=[spec] * 5,
        scratch_shapes=[
            vm((width, cols), bf16),
            vm((tokens, tokens), f32),
            vm((2, n_bits, width, size), bf16),
            vm((2, n_bits, width, size), bf16),
            vm((width, size), f32),
            vm((width, size), bf16),
            vm((width, size), bf16),
            vm((H, tokens, tokens), bf16),
            vm((tokens, width), f32),
            vm((H, tokens, 1), f32),
            vm((tokens, width), bf16),
            vm((tokens, width), f32),
            vm((tokens, width), bf16),
            vm((H, tokens, tokens), bf16),
            vm((width, cols), bf16),
            vm((n_z, rows, cols), bf16),
            vm((n_z, rows, cols), bf16),
            vm((3, n_z, rows, quarter), bf16),
            vm((n_z - 1, rows, quarter), bf16),
            vm((n_z - 1, rows, quarter), bf16),
            vm((rows, quarter), f32),
            vm((more, rows, quarter), bf16),
            vm((more, rows, quarter), bf16),
            vm((rows, cols), bf16),
            dma((2, n_z - 1)), dma((2, n_z - 1)),
            dma((2, n_z - 1)), dma((2, n_z - 1)),
            dma((n_z,)), dma((n_z,)),
            dma((2, n_bits, CHUNKS)), dma((2, n_bits, CHUNKS)),
            dma((n_z,)), dma((n_z,)),
            dma((3, n_z)), dma((3, n_z)),
            dma((n_z - 1,)), dma((n_z - 1,)),
            dma((more,)), dma((more,)),
            dma((3,)), dma((3,)),
            vm((tokens, width), bf16), vm((tokens, width), bf16),
            vm((tokens, width), bf16), vm((tokens, width), bf16),
            vm(block_mask.shape[1:], jnp.int32), dma((6,)),
        ],
        compiler_params=pltpu.CompilerParams(
            collective_id=0, has_side_effects=True, vmem_limit_bytes=60 * 1024 * 1024
        ),
    )(queries[0], keys[0], values[0], out_grad[0], out_weight, block_mask[0])
    outs = pl.pallas_call(
        store,
        out_shape=[jax.ShapeDtypeStruct(o.shape, o.dtype) for o in outs],
        in_specs=[pl.BlockSpec(memory_space=pltpu.HBM)] * 5,
        out_specs=[pl.BlockSpec(memory_space=pltpu.HBM)] * 5,
        scratch_shapes=[vm(o.shape, o.dtype) for o in outs] + [dma((5,)), dma((5,))],
        compiler_params=pltpu.CompilerParams(vmem_limit_bytes=60 * 1024 * 1024),
    )(*outs)
    return tuple(o[None] for o in outs[:4]) + (outs[4],)


def solution(mesh):
    token_spec = P("dp", "seq", None)
    row_spec = P("dp", None)
    return jax.shard_map(
        functools.partial(on_device, mesh.shape["seq"], mesh.shape["dp"]),
        mesh=mesh,
        in_specs=(token_spec,) * 4 + (row_spec, token_spec),
        out_specs=(token_spec,) * 4 + (row_spec,),
        check_vma=False,
    )
```

profile of v0, /device:TPU:0, one launch (start us, length us, event | category | flops | bytes accessed | tf_op | source)
XLA Modules:
  0.0 52.8 jit_solution(17078984292366974566)
XLA Ops:
  0.6 49.5 %shard_map.101 = (bf16[256,1024]{1,0:T(8,128)(2,1)}, bf16[256,1024]{1,0:T(8,128)(2,1)}, bf16[256,1024]{1,0:T(8,128)(2,1)}, bf16[256,1024]{1,0:T(8,128)(2,1)}, f32[128,1024]{1,0:T(8,128)}) custom-call(bf16[256,1024]{1,0:T(8,128)(2,1)} %bitcast.9, bf16[256,1024]{1,0:T(8,128)(2,1)} %bitcast.10, bf16[256,1024]{1,0:T(8,128)(2,1)} %bitcast.11, ...), custom_call_target="tpu_custom_call" | custom-call | tf_op jit(solution)/shard_map/pallas_call | solution.py:360
  50.2 2.6 %shard_map.102 = (bf16[256,1024]{1,0:T(8,128)(2,1)}, bf16[256,1024]{1,0:T(8,128)(2,1)}, bf16[256,1024]{1,0:T(8,128)(2,1)}, bf16[256,1024]{1,0:T(8,128)(2,1)}, f32[128,1024]{1,0:T(8,128)}) custom-call(bf16[256,1024]{1,0:T(8,128)(2,1)} %get-tuple-element.15.refs_0_, bf16[256,1024]{1,0:T(8,128)(2,1)} %get-tuple-element.16.refs_1_, ...), custom_call_target="tpu_custom_call" | custom-call | tf_op jit(solution)/shard_map/pallas_call | solution.py:407
where the time goes:
time: 52.9 us; the launch traced here: 52.8 us
  Pallas kernels  52.1 us (98%)
  between operations  0.64 us (1%)
    pallas_call x1, Pallas kernels, on_device(): pl.pallas_call(functools.partial(kernel, n_seq, n_dp), out_shape=[act, ac...  49.5 us
    pallas_call x1, Pallas kernels, on_device(): pl.pallas_call(store, out_shape=[jax.ShapeDtypeStruct(o.shape, o.dtype) f...  2.61 us

commit v1 on v0

--- a/solution.py
+++ b/solution.py
@@ -333,14 +333,10 @@
 
 
 def store(*refs):
-    src, dst, buf, (load_s, save_s) = refs[:5], refs[5:10], refs[10:15], refs[15:]
-    loads = [pltpu.make_async_copy(src[i], buf[i], load_s.at[i]) for i in range(5)]
-    saves = [pltpu.make_async_copy(buf[i], dst[i], save_s.at[i]) for i in range(5)]
-    for c in loads:
+    src, dst, sems = refs[:5], refs[5:10], refs[10]
+    saves = [pltpu.make_async_copy(src[i], dst[i], sems.at[i]) for i in range(5)]
+    for c in saves:
         c.start()
-    for i in range(5):
-        loads[i].wait()
-        saves[i].start()
     for c in saves:
         c.wait()
 
@@ -359,7 +355,7 @@
     spec = pl.BlockSpec(memory_space=pltpu.VMEM)
     outs = pl.pallas_call(
         functools.partial(kernel, n_seq, n_dp),
-        out_shape=[act, act, act, act, jax.ShapeDtypeStruct((rows, cols), f32)],
+        out_shape=[vm((tokens, width), bf16)] * 4 + [vm((rows, cols), f32)],
         in_specs=[pl.BlockSpec(memory_space=pltpu.HBM)] * 6,
         out_specs=[spec] * 5,
         scratch_shapes=[
@@ -401,16 +397,16 @@
             vm(block_mask.shape[1:], jnp.int32), dma((6,)),
         ],
         compiler_params=pltpu.CompilerParams(
-            collective_id=0, has_side_effects=True, vmem_limit_bytes=60 * 1024 * 1024
+            collective_id=0, has_side_effects=True, vmem_limit_bytes=40 * 1024 * 1024
         ),
-    )(queries[0], keys[0], values[0], out_grad[0], out_weight, block_mask[0])
+    )(*[pltpu.with_memory_space_constraint(a, pltpu.HBM) for a in (queries[0], keys[0], values[0], out_grad[0], out_weight, block_mask[0])])
     outs = pl.pallas_call(
         store,
         out_shape=[jax.ShapeDtypeStruct(o.shape, o.dtype) for o in outs],
-        in_specs=[pl.BlockSpec(memory_space=pltpu.HBM)] * 5,
+        in_specs=[spec] * 5,
         out_specs=[pl.BlockSpec(memory_space=pltpu.HBM)] * 5,
-        scratch_shapes=[vm(o.shape, o.dtype) for o in outs] + [dma((5,)), dma((5,))],
-        compiler_params=pltpu.CompilerParams(vmem_limit_bytes=60 * 1024 * 1024),
+        scratch_shapes=[dma((5,))],
+        compiler_params=pltpu.CompilerParams(vmem_limit_bytes=4 * 1024 * 1024),
     )(*outs)
     return tuple(o[None] for o in outs[:4]) + (outs[4],)
 

time: 52.9 us -> 50.4 us (0.953)
  Pallas kernels: 52.1 us -> 49.6 us
    pallas_call x1, Pallas kernels: 49.5 us -> 48 us  [on_device(): pl.pallas_call(functools.partial(kernel, n_seq, n_dp), out_shape=[vm((tok...]
    pallas_call x1, Pallas kernels: 2.61 us -> 1.53 us  [on_device(): pl.pallas_call(store, out_shape=[jax.ShapeDtypeStruct(o.shape, o.dtype) f...]
where the time goes in v1:
time: 50.4 us; the launch traced here: 50.2 us
  Pallas kernels  49.6 us (98%)
  between operations  0.64 us (1%)
    pallas_call x1, Pallas kernels, on_device(): pl.pallas_call(functools.partial(kernel, n_seq, n_dp), out_shape=[vm((tok...  48 us
    pallas_call x1, Pallas kernels, on_device(): pl.pallas_call(store, out_shape=[jax.ShapeDtypeStruct(o.shape, o.dtype) f...  1.53 us

profile of v1, /device:TPU:0, one launch (start us, length us, event | category | flops | bytes accessed | tf_op | source)
XLA Modules:
  0.0 50.2 jit_solution(11492909459067769638)
XLA Ops:
  0.6 48.0 %shard_map.101 = (bf16[256,1024]{1,0:T(8,128)(2,1)S(1)}, bf16[256,1024]{1,0:T(8,128)(2,1)S(1)}, bf16[256,1024]{1,0:T(8,128)(2,1)S(1)}, bf16[256,1024]{1,0:T(8,128)(2,1)S(1)}, f32[128,1024]{1,0:T(8,128)S(1)}) custom-call(bf16[256,1024]{1,0:T(8,128)(2,1)} %bitcast.9, bf16[256,1024]{1,0:T(8,128)(2,1)} %bitcast.10, bf16[256,1024]{1,0:T(8,128)(2,1)} %bitcast.11, ...), custom_call_target="tpu_custom_call" | custom-call | tf_op jit(solution)/shard_map/pallas_call | solution.py:356
  48.7 1.5 %shard_map.102 = (bf16[256,1024]{1,0:T(8,128)(2,1)}, bf16[256,1024]{1,0:T(8,128)(2,1)}, bf16[256,1024]{1,0:T(8,128)(2,1)}, bf16[256,1024]{1,0:T(8,128)(2,1)}, f32[128,1024]{1,0:T(8,128)}) custom-call(bf16[256,1024]{1,0:T(8,128)(2,1)S(1)} %get-tuple-element.15.refs_0_, bf16[256,1024]{1,0:T(8,128)(2,1)S(1)} %get-tuple-element.16.refs_1_, ...), custom_call_target="tpu_custom_call" | custom-call | tf_op jit(solution)/shard_map/pallas_call | solution.py:403

commit v2 on v1

--- a/solution.py
+++ b/solution.py
@@ -30,15 +30,12 @@
     return lax.dot_general(a, b, (((da,), (db,)), ((), ())), preferred_element_type=f32)
 
 
-def over_heads(lo, hi, fn):
-    if hi <= lo:
-        return
-
-    def body(h, c):
-        fn(h)
+def over_heads(first, count, fn):
+    def body(i, c):
+        fn(first + i)
         return c
 
-    lax.fori_loop(lo, hi, body, 0, unroll=UNROLL)
+    lax.fori_loop(0, count, body, 0, unroll=min(UNROLL, count))
 
 
 def visibility(mask, tokens):
@@ -63,7 +60,8 @@
     n_seq, n_dp, q_hbm, k_hbm, v_hbm, g_hbm, w_ref, mask_hbm,
     out_ref, qg_ref, kg_ref, vg_ref, wg_ref,
     w_full, vis_ref, s_out, s_in, acc, prior, later, wts, attn, inv, normed,
-    dnormed, dattn, dsc, term, a_in, u_out, x_in, z_out, z_in, z_own, r_out, r_in, f_out,
+    dnormed, dattn, dsc, term, a_in, u_out, first_in, mid_out, second_in, z_out, z_in, z_own,
+    r_out, r_in, f_all,
     w1_s, w1_r, w2_s, w2_r, w3_s, w3_r, st_s, st_r, a_s, a_r, x_s, x_r, z_s, z_r, r_s, r_r,
     f_s, f_r, q_ref, k_ref, v_ref, g_ref, mask_ref, in_s,
 ):
@@ -73,17 +71,18 @@
     rows = w_ref.shape[0]
     cols = w_ref.shape[1]
     quarter = cols // QUAD
+    eighth = quarter // 2
     n_bits = n_seq.bit_length() - 1
     s = lax.axis_index("seq")
     d = lax.axis_index("dp")
     z = lax.div(d, 2)
     core = lax.rem(d, 2)
-    s4 = lax.rem(s, QUAD)
     peer = flip(d, 1)
-    seq_peer = {j: s for j in (1, 2, 3)}
-    seq_peer[1] = flip(s, 1)
-    seq_peer[2] = flip(s, 2)
-    seq_peer[3] = flip(flip(s, 1), 2)
+    seq_peer = {1: flip(s, 1), 2: flip(s, 2), 3: flip(flip(s, 1), 2)}
+    bits = (bit(s, 1), bit(s, 2))
+    zb = n_z // CHUNKS
+    half = width // CHUNKS
+    per = H // CHUNKS
 
     def qcols(seq_index):
         return pl.ds(pl.multiple_of(lax.rem(seq_index, QUAD) * quarter, quarter), quarter)
@@ -99,6 +98,15 @@
 
     def down(k):
         return lax.rem(z + n_z - k, n_z)
+
+    def chunk_at(i):
+        return lax.rem(lax.div(z, zb) + 1 + i, CHUNKS)
+
+    def chunk(i):
+        return pl.ds(pl.multiple_of(chunk_at(i) * half, half), half)
+
+    def heads_of(i, fn):
+        over_heads(chunk_at(i) * per, per, fn)
 
     def rc(src, dst, ss, rs, dev):
         return pltpu.make_async_remote_copy(
@@ -108,10 +116,13 @@
 
     sent = []
 
-    def go(*a):
+    def go(*a, when=None):
         c = rc(*a)
-        c.start()
-        sent.append(c)
+        if when is None:
+            c.start()
+        else:
+            pl.when(when)(c.start)
+        sent.append((c, when))
 
     def arrive(dst, ss, rs, dev):
         rc(dst, dst, ss, rs, dev).wait_recv()
@@ -130,6 +141,7 @@
     partners += [(s, up(i) * 2 + core) for i in range(1, n_z)]
     for p in partners:
         pl.semaphore_signal(barrier, inc=1, device_id=p, device_id_type=MESH)
+    acc[...] = jnp.zeros_like(acc)
     pl.semaphore_wait(barrier, len(partners))
 
     own_q = [qcols(s), qcols(seq_peer[3])]
@@ -143,39 +155,57 @@
     loads["k"].wait()
     loads["v"].wait()
 
-    half = width // CHUNKS
-
-    def chunk(c):
-        return pl.ds(c * half, half)
-
-    def send_state(way, b, c):
+    def roles(way, b):
+        own = bit(s, 1 << b)
+        above = lax.div(s, 2 << b)
+        last = (n_seq >> (b + 1)) - 1
+        takes = own == 1 if way == 0 else own == 0
+        if last == 0:
+            return takes, None
+        return takes, above != last if way == 0 else above != 0
+
+    def send_state(way, b, i, when):
         go(
-            s_out.at[way, b, chunk(c)], s_in.at[way, b, chunk(c)],
-            st_s.at[way, b, c], st_r.at[way, b, c], (flip(s, 1 << b), d),
+            s_out.at[way, b, chunk(i)], s_in.at[way, b, chunk(i)],
+            st_s.at[way, b, i], st_r.at[way, b, i], (flip(s, 1 << b), d), when=when,
         )
 
-    def state_step(way, b, c):
-        arrive(s_in.at[way, b, chunk(c)], st_s.at[way, b, c], st_r.at[way, b, c], (flip(s, 1 << b), d))
-        got = s_in[way, b, chunk(c)].astype(f32)
-        if b + 1 < n_bits:
-            s_out[way, b + 1, chunk(c)] = (s_out[way, b, chunk(c)].astype(f32) + got).astype(bf16)
-            send_state(way, b + 1, c)
-        own_bit = bit(s, 1 << b)
-        use = (own_bit if way == 0 else 1 - own_bit).astype(f32)
-        if b == 0:
-            acc[chunk(c)] = got * use
+    def first_state(way, i):
+        takes, more = roles(way, 0)
+        gives = jnp.logical_not(takes)
+        send_state(way, 0, i, gives if more is None else jnp.logical_or(gives, more))
+
+    def state_step(way, b, i):
+        takes, more = roles(way, b)
+
+        def receive():
+            arrive(
+                s_in.at[way, b, chunk(i)], st_s.at[way, b, i], st_r.at[way, b, i],
+                (flip(s, 1 << b), d),
+            )
+
+        def pass_on():
+            total = s_out[way, b, chunk(i)].astype(f32) + s_in[way, b, chunk(i)].astype(f32)
+            s_out[way, b + 1, chunk(i)] = total.astype(bf16)
+
+        def take():
+            acc[chunk(i)] += s_in[way, b, chunk(i)].astype(f32)
+
+        if more is None:
+            pl.when(takes)(receive)
         else:
-            acc[chunk(c)] += got * use
-
-    per = H // CHUNKS
-    for c in range(CHUNKS):
-
-        def make_state(h):
-            st = mm(k_ref[:, hcols(h)], v_ref[:, hcols(h)], 0, 0)
-            s_out[0, 0, hcols(h)] = st.astype(bf16)
-
-        over_heads(c * per, (c + 1) * per, make_state)
-        send_state(0, 0, c)
+            pl.when(jnp.logical_or(takes, more))(receive)
+            pl.when(more)(pass_on)
+            send_state(way, b + 1, i, more)
+        pl.when(takes)(take)
+
+    def make_state(h):
+        st = mm(k_ref[:, hcols(h)], v_ref[:, hcols(h)], 0, 0)
+        s_out[0, 0, hcols(h)] = st.astype(bf16)
+
+    for i in range(CHUNKS):
+        heads_of(i, make_state)
+        first_state(0, i)
 
     loads["q"].wait()
     loads["m"].wait()
@@ -187,10 +217,11 @@
         wts[h] = wt
         attn[:, hcols(h)] = mm(wt, v_ref[:, hcols(h)], 1, 0)
 
-    over_heads(0, H, local_attn)
-
-    for c in range(CHUNKS):
-        state_step(0, 0, c)
+    for i in range(CHUNKS):
+        heads_of(i, local_attn)
+
+    for i in range(CHUNKS):
+        state_step(0, 0, i)
 
     for i in range(1, n_z):
         src = down(i) * 2 + core
@@ -200,11 +231,6 @@
                 w_full.at[brow(src), own_q[0]], w_full.at[brow(src), own_q[0]],
                 w2_s.at[j - 1, i - 1], w2_r.at[j - 1, i - 1], (seq_peer[j], d),
             )
-
-    for b in range(1, n_bits):
-        for c in range(CHUNKS):
-            state_step(0, b, c)
-    prior[...] = acc[...].astype(bf16)
 
     loads["g"].wait()
     loads["w"].wait()
@@ -219,13 +245,69 @@
         normed[:, hcols(h)] = n
         term[hcols(h), :] = mm(n, g_ref[...], 0, 0).astype(bf16)
 
-    over_heads(0, H, finish_attn)
-
-    for i in range(n_z):
+    def sub(side, i0, i1):
+        return 2 * quarter * side + i0 * quarter + i1 * eighth
+
+    def lanes(start, length):
+        return pl.ds(pl.multiple_of(start, eighth), length)
+
+    def swap_cores(i):
         zz = up(i + 1)
-        go(
-            term.at[brow(zz * 2 + 1 - core)], a_in.at[zz], a_s.at[i], a_r.at[i], (s, peer)
-        )
+        go(term.at[brow(zz * 2 + 1 - core)], a_in.at[i], a_s.at[i], a_r.at[i], (s, peer))
+
+    def first_cut(i):
+        zz = up(i + 1)
+        arrive(a_in.at[i], a_s.at[i], a_r.at[i], (s, peer))
+        u_out[i] = (term[brow(zz * 2 + core), :].astype(f32) + a_in[i].astype(f32)).astype(bf16)
+        for side in (0, 1):
+            go(
+                u_out.at[i, :, lanes(sub(side, 1 - bits[side], 0), quarter)], first_in.at[side, i],
+                x_s.at[0, side, i], x_r.at[0, side, i], (seq_peer[1 + side], d),
+            )
+
+    def second_cut(i):
+        for side in (0, 1):
+            arrive(first_in.at[side, i], x_s.at[0, side, i], x_r.at[0, side, i], (seq_peer[1 + side], d))
+            other = 1 - bits[1 - side]
+            got = first_in[side, i, :, lanes(other * eighth, eighth)].astype(f32)
+            own = u_out[i, :, lanes(sub(side, bits[side], other), eighth)].astype(f32)
+            mid_out[side, i] = (own + got).astype(bf16)
+            go(
+                mid_out.at[side, i], second_in.at[side, i],
+                x_s.at[1, side, i], x_r.at[1, side, i], (seq_peer[2 - side], d),
+            )
+
+    def z_step(i):
+        zz = up(i + 1)
+        for side in (0, 1):
+            arrive(second_in.at[side, i], x_s.at[1, side, i], x_r.at[1, side, i], (seq_peer[2 - side], d))
+            mine = bits[1 - side]
+            total = u_out[i, :, lanes(sub(side, bits[side], mine), eighth)].astype(f32)
+            total = total + first_in[side, i, :, lanes(mine * eighth, eighth)].astype(f32)
+            total = total + second_in[side, i].astype(f32)
+            if i < n_z - 1:
+                z_out[i, :, side * eighth:(side + 1) * eighth] = total.astype(bf16)
+            else:
+                z_own[:, side * eighth:(side + 1) * eighth] = total
+        if i < n_z - 1:
+            go(z_out.at[i], z_in.at[i], z_s.at[i], z_r.at[i], (s, zz * 2 + core))
+
+    def blocks_at(i):
+        if zb == 1:
+            return [i]
+        return list(range(n_z)) if i == CHUNKS - 1 else []
+
+    for i in range(CHUNKS):
+        for b in range(1, n_bits):
+            state_step(0, b, i)
+        prior[chunk(i)] = acc[chunk(i)].astype(bf16)
+        acc[chunk(i)] = jnp.zeros((half, size), f32)
+        heads_of(i, finish_attn)
+        for j in blocks_at(i):
+            swap_cores(j)
+        if i >= 1:
+            for j in blocks_at(i - 1):
+                first_cut(j)
 
     for i in range(1, n_z):
         src = down(i) * 2 + core
@@ -237,19 +319,8 @@
             )
         go(w_full.at[brow(src)], w_full.at[brow(src)], w3_s.at[i], w3_r.at[i], (s, peer))
 
-    for i in range(n_z):
-        zz = up(i + 1)
-        arrive(a_in.at[zz], a_s.at[i], a_r.at[i], (s, peer))
-        u_out[zz] = (term[brow(zz * 2 + core), :].astype(f32) + a_in[zz].astype(f32)).astype(bf16)
-        for j in (1, 2, 3):
-            go(
-                u_out.at[zz, :, qcols(seq_peer[j])], x_in.at[j - 1, zz],
-                x_s.at[j - 1, i], x_r.at[j - 1, i], (seq_peer[j], d),
-            )
-
-    for i in range(n_z):
-        src = down(i) * 2 + 1 - core
-        arrive(w_full.at[brow(src)], w3_s.at[i], w3_r.at[i], (s, peer))
+    for j in blocks_at(CHUNKS - 1):
+        first_cut(j)
 
     def grad_norm(h):
         dn = mm(g_ref[...], w_full[hcols(h), :], 1, 1)
@@ -258,21 +329,18 @@
         dattn[:, hcols(h)] = da
         s_out[1, 0, hcols(h)] = mm(q_ref[:, hcols(h)], da, 0, 0).astype(bf16)
 
-    for c in range(CHUNKS):
-        over_heads(c * per, (c + 1) * per, grad_norm)
-        send_state(1, 0, c)
-
-    def z_step(i):
-        zz = up(i + 1)
-        total = u_out[zz, :, qcols(s)].astype(f32)
-        for j in (1, 2, 3):
-            arrive(x_in.at[j - 1, zz], x_s.at[j - 1, i], x_r.at[j - 1, i], (seq_peer[j], d))
-            total = total + x_in[j - 1, zz].astype(f32)
-        if i < n_z - 1:
-            z_out[i] = total.astype(bf16)
-            go(z_out.at[i], z_in.at[i], z_s.at[i], z_r.at[i], (s, zz * 2 + core))
-        else:
-            z_own[...] = total
+    def parts(i):
+        return range(i * n_z // CHUNKS, (i + 1) * n_z // CHUNKS)
+
+    for i in range(CHUNKS):
+        for j in parts(i):
+            second_cut(j)
+        if i == 0:
+            for j in range(n_z):
+                src = down(j) * 2 + 1 - core
+                arrive(w_full.at[brow(src)], w3_s.at[j], w3_r.at[j], (s, peer))
+        heads_of(i, grad_norm)
+        first_state(1, i)
 
     def make_scores(h):
         ds = (mm(dattn[:, hcols(h)], v_ref[:, hcols(h)], 1, 1) * vis_ref[...]).astype(bf16)
@@ -281,18 +349,18 @@
         qg_ref[:, hcols(h)] = qg.astype(bf16)
         out_ref[:, hcols(h)] = mm(normed[...], w_full[:, hcols(h)], 1, 0).astype(bf16)
 
-    for i in range(n_z):
-        over_heads(i * H // n_z, (i + 1) * H // n_z, make_scores)
-        z_step(i)
-
-    for c in range(CHUNKS):
-        state_step(1, 0, c)
+    for i in range(CHUNKS):
+        heads_of(i, make_scores)
+        for j in parts(i):
+            z_step(j)
+        state_step(1, 0, i)
 
     def local_grads(h):
         attn[:, hcols(h)] = mm(dsc[h], q_ref[:, hcols(h)], 0, 0)
         dnormed[:, hcols(h)] = mm(wts[h], dattn[:, hcols(h)], 0, 0)
 
-    over_heads(0, H, local_grads)
+    for i in range(CHUNKS):
+        heads_of(i, local_grads)
 
     total = z_own[...]
     for i in range(n_z - 1):
@@ -300,22 +368,16 @@
         arrive(z_in.at[i], z_s.at[i], z_r.at[i], (s, src))
         total = total + z_in[i].astype(f32)
     for b in range(2, n_bits):
-        r_out[b - 2] = total.astype(bf16)
+        own = total.astype(bf16)
+        r_out[b - 2] = own
         dev = (flip(s, 1 << b), d)
         go(r_out.at[b - 2], r_in.at[b - 2], r_s.at[b - 2], r_r.at[b - 2], dev)
         arrive(r_in.at[b - 2], r_s.at[b - 2], r_r.at[b - 2], dev)
-        total = total + r_in[b - 2].astype(f32)
-    f_out[:, qcols(s)] = total.astype(bf16)
+        total = own.astype(f32) + r_in[b - 2].astype(f32)
+    place = lax.rem(s, QUAD)
+    f_all[place] = total.astype(bf16)
     for j in (1, 2, 3):
-        go(
-            f_out.at[:, qcols(s)], f_out.at[:, qcols(s)], f_s.at[j - 1], f_r.at[j - 1],
-            (seq_peer[j], d),
-        )
-
-    for b in range(1, n_bits):
-        for c in range(CHUNKS):
-            state_step(1, b, c)
-    later[...] = acc[...].astype(bf16)
+        go(f_all.at[place], f_all.at[place], f_s.at[j - 1], f_r.at[j - 1], (seq_peer[j], d))
 
     def last_grads(h):
         kg = attn[:, hcols(h)] + mm(v_ref[:, hcols(h)], later[hcols(h), :], 1, 1)
@@ -323,13 +385,27 @@
         vg = dnormed[:, hcols(h)] + mm(k_ref[:, hcols(h)], later[hcols(h), :], 1, 0)
         vg_ref[:, hcols(h)] = vg.astype(bf16)
 
-    over_heads(0, H, last_grads)
+    for i in range(CHUNKS):
+        for b in range(1, n_bits):
+            state_step(1, b, i)
+        later[chunk(i)] = acc[chunk(i)].astype(bf16)
+        heads_of(i, last_grads)
 
     for j in (1, 2, 3):
-        arrive(f_out.at[:, qcols(seq_peer[j])], f_s.at[j - 1], f_r.at[j - 1], (seq_peer[j], d))
-    wg_ref[...] = f_out[...].astype(f32) * (1.0 / math.sqrt(n_seq * n_dp * tokens))
-    for c in sent:
-        c.wait_send()
+        there = lax.rem(seq_peer[j], QUAD)
+        arrive(f_all.at[there], f_s.at[j - 1], f_r.at[j - 1], (seq_peer[j], d))
+    scale = 1.0 / math.sqrt(n_seq * n_dp * tokens)
+    for p in range(QUAD):
+        xy = (p % 2, p // 2)
+        for side in (0, 1):
+            at = sub(side, xy[side], xy[1 - side])
+            got = f_all[p, :, side * eighth:(side + 1) * eighth]
+            wg_ref[:, at:at + eighth] = got.astype(f32) * scale
+    for c, when in sent:
+        if when is None:
+            c.wait_send()
+        else:
+            pl.when(when)(c.wait_send)
 
 
 def store(*refs):
@@ -349,6 +425,7 @@
     n_bits = n_seq.bit_length() - 1
     more = max(n_bits - 2, 1)
     quarter = cols // QUAD
+    eighth = quarter // 2
     dma = pltpu.SemaphoreType.DMA
     vm = pltpu.VMEM
     act = jax.ShapeDtypeStruct((tokens, width), bf16)
@@ -376,19 +453,21 @@
             vm((width, cols), bf16),
             vm((n_z, rows, cols), bf16),
             vm((n_z, rows, cols), bf16),
-            vm((3, n_z, rows, quarter), bf16),
+            vm((2, n_z, rows, quarter), bf16),
+            vm((2, n_z, rows, eighth), bf16),
+            vm((2, n_z, rows, eighth), bf16),
             vm((n_z - 1, rows, quarter), bf16),
             vm((n_z - 1, rows, quarter), bf16),
             vm((rows, quarter), f32),
             vm((more, rows, quarter), bf16),
             vm((more, rows, quarter), bf16),
-            vm((rows, cols), bf16),
+            vm((QUAD, rows, quarter), bf16),
             dma((2, n_z - 1)), dma((2, n_z - 1)),
             dma((2, n_z - 1)), dma((2, n_z - 1)),
             dma((n_z,)), dma((n_z,)),
             dma((2, n_bits, CHUNKS)), dma((2, n_bits, CHUNKS)),
             dma((n_z,)), dma((n_z,)),
-            dma((3, n_z)), dma((3, n_z)),
+            dma((2, 2, n_z)), dma((2, 2, n_z)),
             dma((n_z - 1,)), dma((n_z - 1,)),
             dma((more,)), dma((more,)),
             dma((3,)), dma((3,)),

time: 50.4 us -> 44.7 us (0.89)
  Pallas kernels: 49.6 us -> 43.9 us
    pallas_call x1, Pallas kernels: 48 us -> 42.4 us  [on_device(): pl.pallas_call(functools.partial(kernel, n_seq, n_dp), out_shape=[vm((tok...]
where the time goes in v2:
time: 44.7 us; the launch traced here: 44.5 us
  Pallas kernels  43.9 us (98%)
  between operations  0.64 us (1%)
    pallas_call x1, Pallas kernels, on_device(): pl.pallas_call(functools.partial(kernel, n_seq, n_dp), out_shape=[vm((tok...  42.4 us
    pallas_call x1, Pallas kernels, on_device(): pl.pallas_call(store, out_shape=[jax.ShapeDtypeStruct(o.shape, o.dtype) f...  1.53 us

profile of v2, /device:TPU:0, one launch (start us, length us, event | category | flops | bytes accessed | tf_op | source)
XLA Modules:
  0.0 44.5 jit_solution(18249203384957581370)
XLA Ops:
  0.6 42.4 %shard_map.101 = (bf16[256,1024]{1,0:T(8,128)(2,1)S(1)}, bf16[256,1024]{1,0:T(8,128)(2,1)S(1)}, bf16[256,1024]{1,0:T(8,128)(2,1)S(1)}, bf16[256,1024]{1,0:T(8,128)(2,1)S(1)}, f32[128,1024]{1,0:T(8,128)S(1)}) custom-call(bf16[256,1024]{1,0:T(8,128)(2,1)} %bitcast.9, bf16[256,1024]{1,0:T(8,128)(2,1)} %bitcast.10, bf16[256,1024]{1,0:T(8,128)(2,1)} %bitcast.11, ...), custom_call_target="tpu_custom_call" | custom-call | tf_op jit(solution)/shard_map/pallas_call | solution.py:433
  43.0 1.5 %shard_map.102 = (bf16[256,1024]{1,0:T(8,128)(2,1)}, bf16[256,1024]{1,0:T(8,128)(2,1)}, bf16[256,1024]{1,0:T(8,128)(2,1)}, bf16[256,1024]{1,0:T(8,128)(2,1)}, f32[128,1024]{1,0:T(8,128)}) custom-call(bf16[256,1024]{1,0:T(8,128)(2,1)S(1)} %get-tuple-element.15.refs_0_, bf16[256,1024]{1,0:T(8,128)(2,1)S(1)} %get-tuple-element.16.refs_1_, ...), custom_call_target="tpu_custom_call" | custom-call | tf_op jit(solution)/shard_map/pallas_call | solution.py:482

commit v3 on v2

--- a/solution.py
+++ b/solution.py
@@ -60,11 +60,12 @@
     n_seq, n_dp, q_hbm, k_hbm, v_hbm, g_hbm, w_ref, mask_hbm,
     out_ref, qg_ref, kg_ref, vg_ref, wg_ref,
     w_full, vis_ref, s_out, s_in, acc, prior, later, wts, attn, inv, normed,
-    dnormed, dattn, dsc, term, a_in, u_out, first_in, mid_out, second_in, z_out, z_in, z_own,
-    r_out, r_in, f_all,
-    w1_s, w1_r, w2_s, w2_r, w3_s, w3_r, st_s, st_r, a_s, a_r, x_s, x_r, z_s, z_r, r_s, r_r,
-    f_s, f_r, q_ref, k_ref, v_ref, g_ref, mask_ref, in_s,
+    dnormed, dattn, dsc, term, a_in, u_out, *rest,
 ):
+    first_in, mid_out, second_in, rest = rest[:2], rest[2:4], rest[4:6], rest[6:]
+    z_out, z_in, z_own, c_in, c_own, c_got, r_out, r_in, f_all, *rest = rest
+    w1_s, w1_r, w2_s, w2_r, w3_s, w3_r, st_s, st_r, a_s, a_r, x_s, x_r, z_s, z_r, *rest = rest
+    c_s, c_r, t_s, t_r, r_s, r_r, f_s, f_r, q_ref, k_ref, v_ref, g_ref, mask_ref, in_s = rest
     tokens, width = q_ref.shape
     size = width // H
     n_z = n_dp // 2
@@ -72,6 +73,8 @@
     cols = w_ref.shape[1]
     quarter = cols // QUAD
     eighth = quarter // 2
+    hr = rows // 2
+    scale = 1.0 / math.sqrt(n_seq * n_dp * tokens)
     n_bits = n_seq.bit_length() - 1
     s = lax.axis_index("seq")
     d = lax.axis_index("dp")
@@ -145,11 +148,11 @@
     pl.semaphore_wait(barrier, len(partners))
 
     own_q = [qcols(s), qcols(seq_peer[3])]
-    for part in range(2):
+    for qn in range(2):
         for i in range(1, n_z):
             go(
-                w_ref.at[:, own_q[part]], w_full.at[brow(d), own_q[part]],
-                w1_s.at[part, i - 1], w1_r.at[part, i - 1], (s, up(i) * 2 + core),
+                w_ref.at[:, own_q[qn]], w_full.at[brow(d), own_q[qn]],
+                w1_s.at[qn, i - 1], w1_r.at[qn, i - 1], (s, up(i) * 2 + core),
             )
     go(w_ref, w_full.at[brow(d)], w3_s.at[0], w3_r.at[0], (s, peer))
     loads["k"].wait()
@@ -203,7 +206,7 @@
         st = mm(k_ref[:, hcols(h)], v_ref[:, hcols(h)], 0, 0)
         s_out[0, 0, hcols(h)] = st.astype(bf16)
 
-    for i in range(CHUNKS):
+    for i in (0, 1, 2, 3):
         heads_of(i, make_state)
         first_state(0, i)
 
@@ -217,10 +220,10 @@
         wts[h] = wt
         attn[:, hcols(h)] = mm(wt, v_ref[:, hcols(h)], 1, 0)
 
-    for i in range(CHUNKS):
+    for i in (0, 1, 2, 3):
         heads_of(i, local_attn)
 
-    for i in range(CHUNKS):
+    for i in (0, 1, 2, 3):
         state_step(0, 0, i)
 
     for i in range(1, n_z):
@@ -245,11 +248,22 @@
         normed[:, hcols(h)] = n
         term[hcols(h), :] = mm(n, g_ref[...], 0, 0).astype(bf16)
 
-    def sub(side, i0, i1):
-        return 2 * quarter * side + i0 * quarter + i1 * eighth
-
-    def lanes(start, length):
-        return pl.ds(pl.multiple_of(start, eighth), length)
+    starts = (0, quarter)
+    wide = (eighth, quarter)
+    offs = (0, eighth)
+    tail = slice(3 * quarter, 4 * quarter)
+
+    def axes(side, block):
+        turn = lax.rem(block + side, 2) == 0
+        first = jnp.where(turn, seq_peer[1], seq_peer[2]), jnp.where(turn, bits[0], bits[1])
+        second = jnp.where(turn, seq_peer[2], seq_peer[1]), jnp.where(turn, bits[1], bits[0])
+        return first, second
+
+    def lanes(side, b):
+        return pl.ds(pl.multiple_of(starts[side] + b * wide[side], eighth), wide[side])
+
+    def part(b):
+        return pl.ds(pl.multiple_of(b * hr, hr), hr)
 
     def swap_cores(i):
         zz = up(i + 1)
@@ -259,68 +273,73 @@
         zz = up(i + 1)
         arrive(a_in.at[i], a_s.at[i], a_r.at[i], (s, peer))
         u_out[i] = (term[brow(zz * 2 + core), :].astype(f32) + a_in[i].astype(f32)).astype(bf16)
-        for side in (0, 1):
+        for side in (1, 0):
+            (dev, b), _ = axes(side, zz)
             go(
-                u_out.at[i, :, lanes(sub(side, 1 - bits[side], 0), quarter)], first_in.at[side, i],
-                x_s.at[0, side, i], x_r.at[0, side, i], (seq_peer[1 + side], d),
+                u_out.at[i, :, lanes(side, 1 - b)], first_in[side].at[i],
+                x_s.at[0, side, i], x_r.at[0, side, i], (dev, d),
             )
+        if i < n_z - 1:
+            go(u_out.at[i, :, tail], c_in.at[i], c_s.at[i], c_r.at[i], (s, zz * 2 + core))
 
     def second_cut(i):
-        for side in (0, 1):
-            arrive(first_in.at[side, i], x_s.at[0, side, i], x_r.at[0, side, i], (seq_peer[1 + side], d))
-            other = 1 - bits[1 - side]
-            got = first_in[side, i, :, lanes(other * eighth, eighth)].astype(f32)
-            own = u_out[i, :, lanes(sub(side, bits[side], other), eighth)].astype(f32)
-            mid_out[side, i] = (own + got).astype(bf16)
+        for side in (1, 0):
+            (dev, b), (dev2, b2) = axes(side, up(i + 1))
+            arrive(first_in[side].at[i], x_s.at[0, side, i], x_r.at[0, side, i], (dev, d))
+            got = first_in[side][i, part(1 - b2), :].astype(f32)
+            own = u_out[i, part(1 - b2), lanes(side, b)].astype(f32)
+            mid_out[side][i] = (own + got).astype(bf16)
             go(
-                mid_out.at[side, i], second_in.at[side, i],
-                x_s.at[1, side, i], x_r.at[1, side, i], (seq_peer[2 - side], d),
+                mid_out[side].at[i], second_in[side].at[i],
+                x_s.at[1, side, i], x_r.at[1, side, i], (dev2, d),
             )
 
     def z_step(i):
         zz = up(i + 1)
-        for side in (0, 1):
-            arrive(second_in.at[side, i], x_s.at[1, side, i], x_r.at[1, side, i], (seq_peer[2 - side], d))
-            mine = bits[1 - side]
-            total = u_out[i, :, lanes(sub(side, bits[side], mine), eighth)].astype(f32)
-            total = total + first_in[side, i, :, lanes(mine * eighth, eighth)].astype(f32)
-            total = total + second_in[side, i].astype(f32)
+        for side in (1, 0):
+            (_, b), (dev2, b2) = axes(side, zz)
+            arrive(second_in[side].at[i], x_s.at[1, side, i], x_r.at[1, side, i], (dev2, d))
+            total = u_out[i, part(b2), lanes(side, b)].astype(f32)
+            total = total + first_in[side][i, part(b2), :].astype(f32)
+            total = total + second_in[side][i].astype(f32)
+            at = slice(offs[side], offs[side] + wide[side])
             if i < n_z - 1:
-                z_out[i, :, side * eighth:(side + 1) * eighth] = total.astype(bf16)
+                z_out[i, :, at] = total.astype(bf16)
             else:
-                z_own[:, side * eighth:(side + 1) * eighth] = total
+                z_own[:, at] = total
         if i < n_z - 1:
             go(z_out.at[i], z_in.at[i], z_s.at[i], z_r.at[i], (s, zz * 2 + core))
 
-    def blocks_at(i):
-        if zb == 1:
-            return [i]
-        return list(range(n_z)) if i == CHUNKS - 1 else []
-
-    for i in range(CHUNKS):
-        for b in range(1, n_bits):
-            state_step(0, b, i)
-        prior[chunk(i)] = acc[chunk(i)].astype(bf16)
-        acc[chunk(i)] = jnp.zeros((half, size), f32)
-        heads_of(i, finish_attn)
-        for j in blocks_at(i):
-            swap_cores(j)
-        if i >= 1:
-            for j in blocks_at(i - 1):
-                first_cut(j)
-
-    for i in range(1, n_z):
-        src = down(i) * 2 + core
-        arrive(w_full.at[brow(src), own_q[1]], w1_s.at[1, i - 1], w1_r.at[1, i - 1], (s, src))
-        for j in (1, 2):
-            arrive(
-                w_full.at[brow(src), qcols(seq_peer[j])], w2_s.at[j - 1, i - 1],
-                w2_r.at[j - 1, i - 1], (seq_peer[j], d),
-            )
-        go(w_full.at[brow(src)], w_full.at[brow(src)], w3_s.at[i], w3_r.at[i], (s, peer))
-
-    for j in blocks_at(CHUNKS - 1):
-        first_cut(j)
+    halves = (slice(0, hr), slice(hr, 2 * hr))
+
+    def tail_first():
+        total = u_out[n_z - 1, :, tail].astype(f32)
+        for i in range(n_z - 1):
+            arrive(c_in.at[i], c_s.at[i], c_r.at[i], (s, down(i + 1) * 2 + core))
+            total = total + c_in[i].astype(f32)
+        c_own[0] = total.astype(bf16)
+        for h in (0, 1):
+            go(c_own.at[0, halves[h]], c_got.at[0, halves[h]], t_s.at[0, h], t_r.at[0, h], (seq_peer[1 + h], d))
+
+    def tail_second():
+        for h in (0, 1):
+            arrive(c_got.at[0, halves[h]], t_s.at[0, h], t_r.at[0, h], (seq_peer[1 + h], d))
+            total = c_own[0, halves[h]].astype(f32) + c_got[0, halves[h]].astype(f32)
+            c_own[1, halves[h]] = total.astype(bf16)
+            go(c_own.at[1, halves[h]], c_got.at[1, halves[h]], t_s.at[1, h], t_r.at[1, h], (seq_peer[2 - h], d))
+
+    def tail_last():
+        for h in (0, 1):
+            arrive(c_got.at[1, halves[h]], t_s.at[1, h], t_r.at[1, h], (seq_peer[2 - h], d))
+        total = c_own[1].astype(f32) + c_got[1].astype(f32)
+        for b in range(2, n_bits):
+            own = total.astype(bf16)
+            c_own[b] = own
+            dev = (flip(s, 1 << b), d)
+            go(c_own.at[b], c_got.at[b], t_s.at[b, 0], t_r.at[b, 0], dev)
+            arrive(c_got.at[b], t_s.at[b, 0], t_r.at[b, 0], dev)
+            total = own.astype(f32) + c_got[b].astype(f32)
+        wg_ref[:, tail] = total * scale
 
     def grad_norm(h):
         dn = mm(g_ref[...], w_full[hcols(h), :], 1, 1)
@@ -332,15 +351,83 @@
     def parts(i):
         return range(i * n_z // CHUNKS, (i + 1) * n_z // CHUNKS)
 
-    for i in range(CHUNKS):
+    def offsets_of(i):
+        if zb == 1:
+            return [CHUNKS - 1 - i]
+        return list(range(n_z)) if i == CHUNKS - 1 else []
+
+    def rows_over(i):
+        for k in offsets_of(i):
+            if k == 0:
+                continue
+            src = down(k) * 2 + core
+            arrive(w_full.at[brow(src), own_q[1]], w1_s.at[1, k - 1], w1_r.at[1, k - 1], (s, src))
+            for j in (1, 2):
+                arrive(
+                    w_full.at[brow(src), qcols(seq_peer[j])], w2_s.at[j - 1, k - 1],
+                    w2_r.at[j - 1, k - 1], (seq_peer[j], d),
+                )
+            go(w_full.at[brow(src)], w_full.at[brow(src)], w3_s.at[k], w3_r.at[k], (s, peer))
+
+    def rows_here(i):
+        for k in offsets_of(i):
+            src = down(k) * 2 + 1 - core
+            arrive(w_full.at[brow(src)], w3_s.at[k], w3_r.at[k], (s, peer))
+
+    def cut_again(i):
         for j in parts(i):
             second_cut(j)
-        if i == 0:
-            for j in range(n_z):
-                src = down(j) * 2 + 1 - core
-                arrive(w_full.at[brow(src)], w3_s.at[j], w3_r.at[j], (s, peer))
-        heads_of(i, grad_norm)
-        first_state(1, i)
+
+    def last_cut(i):
+        for j in parts(i):
+            z_step(j)
+
+    def every(i, last):
+        if zb == 1:
+            return [i]
+        return list(range(n_z)) if last else []
+
+    def finish(i, last=False):
+        for b in range(1, n_bits):
+            state_step(0, b, i)
+        prior[chunk(i)] = acc[chunk(i)].astype(bf16)
+        acc[chunk(i)] = jnp.zeros((half, size), f32)
+        heads_of(i, finish_attn)
+        for j in every(i, last):
+            swap_cores(j)
+
+    def cut_first(i, last=False):
+        for j in every(i, last):
+            first_cut(j)
+
+    finish(0)
+    finish(1)
+    cut_first(0)
+    finish(2)
+    cut_first(1)
+    finish(3, True)
+    cut_first(2)
+    rows_over(2)
+    rows_over(3)
+    rows_here(3)
+    heads_of(3, grad_norm)
+    first_state(1, 3)
+    cut_first(3, True)
+    rows_over(1)
+    cut_again(0)
+    rows_here(2)
+    heads_of(2, grad_norm)
+    first_state(1, 2)
+    rows_over(0)
+    cut_again(1)
+    rows_here(1)
+    heads_of(1, grad_norm)
+    first_state(1, 1)
+    cut_again(2)
+    rows_here(0)
+    heads_of(0, grad_norm)
+    first_state(1, 0)
+    cut_again(3)
 
     def make_scores(h):
         ds = (mm(dattn[:, hcols(h)], v_ref[:, hcols(h)], 1, 1) * vis_ref[...]).astype(bf16)
@@ -349,17 +436,26 @@
         qg_ref[:, hcols(h)] = qg.astype(bf16)
         out_ref[:, hcols(h)] = mm(normed[...], w_full[:, hcols(h)], 1, 0).astype(bf16)
 
-    for i in range(CHUNKS):
-        heads_of(i, make_scores)
-        for j in parts(i):
-            z_step(j)
-        state_step(1, 0, i)
+    heads_of(3, make_scores)
+    last_cut(0)
+    state_step(1, 0, 3)
+    heads_of(2, make_scores)
+    last_cut(1)
+    tail_first()
+    state_step(1, 0, 2)
+    heads_of(1, make_scores)
+    last_cut(2)
+    state_step(1, 0, 1)
+    heads_of(0, make_scores)
+    last_cut(3)
+    state_step(1, 0, 0)
+    tail_second()
 
     def local_grads(h):
         attn[:, hcols(h)] = mm(dsc[h], q_ref[:, hcols(h)], 0, 0)
         dnormed[:, hcols(h)] = mm(wts[h], dattn[:, hcols(h)], 0, 0)
 
-    for i in range(CHUNKS):
+    for i in reversed(range(CHUNKS)):
         heads_of(i, local_grads)
 
     total = z_own[...]
@@ -379,13 +475,15 @@
     for j in (1, 2, 3):
         go(f_all.at[place], f_all.at[place], f_s.at[j - 1], f_r.at[j - 1], (seq_peer[j], d))
 
+    tail_last()
+
     def last_grads(h):
         kg = attn[:, hcols(h)] + mm(v_ref[:, hcols(h)], later[hcols(h), :], 1, 1)
         kg_ref[:, hcols(h)] = kg.astype(bf16)
         vg = dnormed[:, hcols(h)] + mm(k_ref[:, hcols(h)], later[hcols(h), :], 1, 0)
         vg_ref[:, hcols(h)] = vg.astype(bf16)
 
-    for i in range(CHUNKS):
+    for i in reversed(range(CHUNKS)):
         for b in range(1, n_bits):
             state_step(1, b, i)
         later[chunk(i)] = acc[chunk(i)].astype(bf16)
@@ -394,13 +492,12 @@
     for j in (1, 2, 3):
         there = lax.rem(seq_peer[j], QUAD)
         arrive(f_all.at[there], f_s.at[j - 1], f_r.at[j - 1], (seq_peer[j], d))
-    scale = 1.0 / math.sqrt(n_seq * n_dp * tokens)
     for p in range(QUAD):
-        xy = (p % 2, p // 2)
         for side in (0, 1):
-            at = sub(side, xy[side], xy[1 - side])
-            got = f_all[p, :, side * eighth:(side + 1) * eighth]
-            wg_ref[:, at:at + eighth] = got.astype(f32) * scale
+            turn = lax.rem(z + side, 2) == 0
+            b, b2 = jnp.where(turn, p % 2, p // 2), jnp.where(turn, p // 2, p % 2)
+            got = f_all[p, :, offs[side]:offs[side] + wide[side]]
+            wg_ref[part(b2), lanes(side, b)] = got.astype(f32) * scale
     for c, when in sent:
         if when is None:
             c.wait_send()
@@ -426,6 +523,8 @@
     more = max(n_bits - 2, 1)
     quarter = cols // QUAD
     eighth = quarter // 2
+    kept = quarter + eighth
+    half_rows = rows // 2
     dma = pltpu.SemaphoreType.DMA
     vm = pltpu.VMEM
     act = jax.ShapeDtypeStruct((tokens, width), bf16)
@@ -453,15 +552,18 @@
             vm((width, cols), bf16),
             vm((n_z, rows, cols), bf16),
             vm((n_z, rows, cols), bf16),
-            vm((2, n_z, rows, quarter), bf16),
-            vm((2, n_z, rows, eighth), bf16),
-            vm((2, n_z, rows, eighth), bf16),
+            vm((n_z, rows, eighth), bf16), vm((n_z, rows, quarter), bf16),
+            vm((n_z, half_rows, eighth), bf16), vm((n_z, half_rows, quarter), bf16),
+            vm((n_z, half_rows, eighth), bf16), vm((n_z, half_rows, quarter), bf16),
+            vm((n_z - 1, half_rows, kept), bf16),
+            vm((n_z - 1, half_rows, kept), bf16),
+            vm((half_rows, kept), f32),
             vm((n_z - 1, rows, quarter), bf16),
-            vm((n_z - 1, rows, quarter), bf16),
-            vm((rows, quarter), f32),
-            vm((more, rows, quarter), bf16),
-            vm((more, rows, quarter), bf16),
-            vm((QUAD, rows, quarter), bf16),
+            vm((n_bits, rows, quarter), bf16),
+            vm((n_bits, rows, quarter), bf16),
+            vm((more, half_rows, kept), bf16),
+            vm((more, half_rows, kept), bf16),
+            vm((QUAD, half_rows, kept), bf16),
             dma((2, n_z - 1)), dma((2, n_z - 1)),
             dma((2, n_z - 1)), dma((2, n_z - 1)),
             dma((n_z,)), dma((n_z,)),
@@ -469,6 +571,8 @@
             dma((n_z,)), dma((n_z,)),
             dma((2, 2, n_z)), dma((2, 2, n_z)),
             dma((n_z - 1,)), dma((n_z - 1,)),
+            dma((n_z - 1,)), dma((n_z - 1,)),
+            dma((n_bits, 2)), dma((n_bits, 2)),
             dma((more,)), dma((more,)),
             dma((3,)), dma((3,)),
             vm((tokens, width), bf16), vm((tokens, width), bf16),

time: 44.7 us -> 42.3 us (0.946)
  Pallas kernels: 43.9 us -> 41.5 us
    pallas_call x1, Pallas kernels: 42.4 us -> 40 us  [on_device(): pl.pallas_call(functools.partial(kernel, n_seq, n_dp), out_shape=[vm((tok...]
where the time goes in v3:
time: 42.3 us; the launch traced here: 42.2 us
  Pallas kernels  41.5 us (98%)
  between operations  0.64 us (2%)
    pallas_call x1, Pallas kernels, on_device(): pl.pallas_call(functools.partial(kernel, n_seq, n_dp), out_shape=[vm((tok...  40 us
    pallas_call x1, Pallas kernels, on_device(): pl.pallas_call(store, out_shape=[jax.ShapeDtypeStruct(o.shape, o.dtype) f...  1.53 us

profile of v3, /device:TPU:0, one launch (start us, length us, event | category | flops | bytes accessed | tf_op | source)
XLA Modules:
  0.0 42.2 jit_solution(177125965809616140)
XLA Ops:
  0.6 40.0 %shard_map.101 = (bf16[256,1024]{1,0:T(8,128)(2,1)S(1)}, bf16[256,1024]{1,0:T(8,128)(2,1)S(1)}, bf16[256,1024]{1,0:T(8,128)(2,1)S(1)}, bf16[256,1024]{1,0:T(8,128)(2,1)S(1)}, f32[128,1024]{1,0:T(8,128)S(1)}) custom-call(bf16[256,1024]{1,0:T(8,128)(2,1)} %bitcast.9, bf16[256,1024]{1,0:T(8,128)(2,1)} %bitcast.10, bf16[256,1024]{1,0:T(8,128)(2,1)} %bitcast.11, ...), custom_call_target="tpu_custom_call" | custom-call | tf_op jit(solution)/shard_map/pallas_call | solution.py:532
  40.6 1.5 %shard_map.102 = (bf16[256,1024]{1,0:T(8,128)(2,1)}, bf16[256,1024]{1,0:T(8,128)(2,1)}, bf16[256,1024]{1,0:T(8,128)(2,1)}, bf16[256,1024]{1,0:T(8,128)(2,1)}, f32[128,1024]{1,0:T(8,128)}) custom-call(bf16[256,1024]{1,0:T(8,128)(2,1)S(1)} %get-tuple-element.15.refs_0_, bf16[256,1024]{1,0:T(8,128)(2,1)S(1)} %get-tuple-element.16.refs_1_, ...), custom_call_target="tpu_custom_call" | custom-call | tf_op jit(solution)/shard_map/pallas_call | solution.py:586

commit v4 on v3

--- a/solution.py
+++ b/solution.py
@@ -167,39 +167,50 @@
             return takes, None
         return takes, above != last if way == 0 else above != 0
 
-    def send_state(way, b, i, when):
+    def head_rows(i, k):
+        return hcols(chunk_at(i) * per + k)
+
+    def send_state(way, b, i, k, when):
         go(
-            s_out.at[way, b, chunk(i)], s_in.at[way, b, chunk(i)],
-            st_s.at[way, b, i], st_r.at[way, b, i], (flip(s, 1 << b), d), when=when,
+            s_out.at[way, b, head_rows(i, k)], s_in.at[way, b, head_rows(i, k)],
+            st_s.at[way, b, i * per + k], st_r.at[way, b, i * per + k], (flip(s, 1 << b), d),
+            when=when,
         )
 
-    def first_state(way, i):
+    def first_state(way, i, fn):
         takes, more = roles(way, 0)
         gives = jnp.logical_not(takes)
-        send_state(way, 0, i, gives if more is None else jnp.logical_or(gives, more))
+        for k in range(per):
+            over_heads(chunk_at(i) * per + k, 1, fn)
+            send_state(way, 0, i, k, gives if more is None else jnp.logical_or(gives, more))
 
     def state_step(way, b, i):
+        for k in range(per):
+            head_step(way, b, i, k)
+
+    def head_step(way, b, i, k):
         takes, more = roles(way, b)
+        at = head_rows(i, k)
 
         def receive():
             arrive(
-                s_in.at[way, b, chunk(i)], st_s.at[way, b, i], st_r.at[way, b, i],
+                s_in.at[way, b, at], st_s.at[way, b, i * per + k], st_r.at[way, b, i * per + k],
                 (flip(s, 1 << b), d),
             )
 
         def pass_on():
-            total = s_out[way, b, chunk(i)].astype(f32) + s_in[way, b, chunk(i)].astype(f32)
-            s_out[way, b + 1, chunk(i)] = total.astype(bf16)
+            total = s_out[way, b, at].astype(f32) + s_in[way, b, at].astype(f32)
+            s_out[way, b + 1, at] = total.astype(bf16)
 
         def take():
-            acc[chunk(i)] += s_in[way, b, chunk(i)].astype(f32)
+            acc[at] += s_in[way, b, at].astype(f32)
 
         if more is None:
             pl.when(takes)(receive)
         else:
             pl.when(jnp.logical_or(takes, more))(receive)
             pl.when(more)(pass_on)
-            send_state(way, b + 1, i, more)
+            send_state(way, b + 1, i, k, more)
         pl.when(takes)(take)
 
     def make_state(h):
@@ -207,8 +218,7 @@
         s_out[0, 0, hcols(h)] = st.astype(bf16)
 
     for i in (0, 1, 2, 3):
-        heads_of(i, make_state)
-        first_state(0, i)
+        first_state(0, i, make_state)
 
     loads["q"].wait()
     loads["m"].wait()
@@ -410,23 +420,19 @@
     rows_over(2)
     rows_over(3)
     rows_here(3)
-    heads_of(3, grad_norm)
-    first_state(1, 3)
+    first_state(1, 3, grad_norm)
     cut_first(3, True)
     rows_over(1)
     cut_again(0)
     rows_here(2)
-    heads_of(2, grad_norm)
-    first_state(1, 2)
+    first_state(1, 2, grad_norm)
     rows_over(0)
     cut_again(1)
     rows_here(1)
-    heads_of(1, grad_norm)
-    first_state(1, 1)
+    first_state(1, 1, grad_norm)
     cut_again(2)
     rows_here(0)
-    heads_of(0, grad_norm)
-    first_state(1, 0)
+    first_state(1, 0, grad_norm)
     cut_again(3)
 
     def make_scores(h):
@@ -447,9 +453,9 @@
     last_cut(2)
     state_step(1, 0, 1)
     heads_of(0, make_scores)
+    tail_second()
     last_cut(3)
     state_step(1, 0, 0)
-    tail_second()
 
     def local_grads(h):
         attn[:, hcols(h)] = mm(dsc[h], q_ref[:, hcols(h)], 0, 0)
@@ -472,7 +478,7 @@
         total = own.astype(f32) + r_in[b - 2].astype(f32)
     place = lax.rem(s, QUAD)
     f_all[place] = total.astype(bf16)
-    for j in (1, 2, 3):
+    for j in (3, 1, 2):
         go(f_all.at[place], f_all.at[place], f_s.at[j - 1], f_r.at[j - 1], (seq_peer[j], d))
 
     tail_last()
@@ -567,7 +573,7 @@
             dma((2, n_z - 1)), dma((2, n_z - 1)),
             dma((2, n_z - 1)), dma((2, n_z - 1)),
             dma((n_z,)), dma((n_z,)),
-            dma((2, n_bits, CHUNKS)), dma((2, n_bits, CHUNKS)),
+            dma((2, n_bits, H)), dma((2, n_bits, H)),
             dma((n_z,)), dma((n_z,)),
             dma((2, 2, n_z)), dma((2, 2, n_z)),
             dma((n_z - 1,)), dma((n_z - 1,)),

time: 42.3 us -> 41.7 us (0.986)
  Pallas kernels: 41.5 us -> 40.9 us
    pallas_call x1, Pallas kernels: 40 us -> 39.4 us  [on_device(): pl.pallas_call(functools.partial(kernel, n_seq, n_dp), out_shape=[vm((tok...]
where the time goes in v4:
time: 41.7 us; the launch traced here: 41.6 us
  Pallas kernels  40.9 us (98%)
  between operations  0.64 us (2%)
    pallas_call x1, Pallas kernels, on_device(): pl.pallas_call(functools.partial(kernel, n_seq, n_dp), out_shape=[vm((tok...  39.4 us
    pallas_call x1, Pallas kernels, on_device(): pl.pallas_call(store, out_shape=[jax.ShapeDtypeStruct(o.shape, o.dtype) f...  1.53 us

profile of v4, /device:TPU:0, one launch (start us, length us, event | category | flops | bytes accessed | tf_op | source)
XLA Modules:
  0.0 41.6 jit_solution(1582613280249921055)
XLA Ops:
  0.6 39.4 %shard_map.101 = (bf16[256,1024]{1,0:T(8,128)(2,1)S(1)}, bf16[256,1024]{1,0:T(8,128)(2,1)S(1)}, bf16[256,1024]{1,0:T(8,128)(2,1)S(1)}, bf16[256,1024]{1,0:T(8,128)(2,1)S(1)}, f32[128,1024]{1,0:T(8,128)S(1)}) custom-call(bf16[256,1024]{1,0:T(8,128)(2,1)} %bitcast.9, bf16[256,1024]{1,0:T(8,128)(2,1)} %bitcast.10, bf16[256,1024]{1,0:T(8,128)(2,1)} %bitcast.11, ...), custom_call_target="tpu_custom_call" | custom-call | tf_op jit(solution)/shard_map/pallas_call | solution.py:538
  40.0 1.5 %shard_map.102 = (bf16[256,1024]{1,0:T(8,128)(2,1)}, bf16[256,1024]{1,0:T(8,128)(2,1)}, bf16[256,1024]{1,0:T(8,128)(2,1)}, bf16[256,1024]{1,0:T(8,128)(2,1)}, f32[128,1024]{1,0:T(8,128)}) custom-call(bf16[256,1024]{1,0:T(8,128)(2,1)S(1)} %get-tuple-element.15.refs_0_, bf16[256,1024]{1,0:T(8,128)(2,1)S(1)} %get-tuple-element.16.refs_1_, ...), custom_call_target="tpu_custom_call" | custom-call | tf_op jit(solution)/shard_map/pallas_call | solution.py:592

commit v5 on v4

--- a/solution.py
+++ b/solution.py
@@ -440,6 +440,8 @@
         dsc[h] = ds
         qg = mm(ds, k_ref[:, hcols(h)], 1, 0) + mm(dattn[:, hcols(h)], prior[hcols(h), :], 1, 1)
         qg_ref[:, hcols(h)] = qg.astype(bf16)
+
+    def make_out(h):
         out_ref[:, hcols(h)] = mm(normed[...], w_full[:, hcols(h)], 1, 0).astype(bf16)
 
     heads_of(3, make_scores)
@@ -461,8 +463,6 @@
         attn[:, hcols(h)] = mm(dsc[h], q_ref[:, hcols(h)], 0, 0)
         dnormed[:, hcols(h)] = mm(wts[h], dattn[:, hcols(h)], 0, 0)
 
-    for i in reversed(range(CHUNKS)):
-        heads_of(i, local_grads)
 
     total = z_own[...]
     for i in range(n_z - 1):
@@ -480,6 +480,11 @@
     f_all[place] = total.astype(bf16)
     for j in (3, 1, 2):
         go(f_all.at[place], f_all.at[place], f_s.at[j - 1], f_r.at[j - 1], (seq_peer[j], d))
+
+    for i in range(CHUNKS):
+        heads_of(i, make_out)
+    for i in reversed(range(CHUNKS)):
+        heads_of(i, local_grads)
 
     tail_last()
 

time: 41.7 us -> 41.7 us (level)
  no operation moved by 1% of the time
where the time goes in v5:
time: 41.7 us; the launch traced here: 41.5 us
  Pallas kernels  40.9 us (98%)
  between operations  0.64 us (2%)
    pallas_call x1, Pallas kernels, on_device(): pl.pallas_call(functools.partial(kernel, n_seq, n_dp), out_shape=[vm((tok...  39.3 us
    pallas_call x1, Pallas kernels, on_device(): pl.pallas_call(store, out_shape=[jax.ShapeDtypeStruct(o.shape, o.dtype) f...  1.53 us

profile of v5, /device:TPU:0, one launch (start us, length us, event | category | flops | bytes accessed | tf_op | source)
XLA Modules:
  0.0 41.5 jit_solution(14945594830759760080)
XLA Ops:
  0.6 39.3 %shard_map.101 = (bf16[256,1024]{1,0:T(8,128)(2,1)S(1)}, bf16[256,1024]{1,0:T(8,128)(2,1)S(1)}, bf16[256,1024]{1,0:T(8,128)(2,1)S(1)}, bf16[256,1024]{1,0:T(8,128)(2,1)S(1)}, f32[128,1024]{1,0:T(8,128)S(1)}) custom-call(bf16[256,1024]{1,0:T(8,128)(2,1)} %bitcast.9, bf16[256,1024]{1,0:T(8,128)(2,1)} %bitcast.10, bf16[256,1024]{1,0:T(8,128)(2,1)} %bitcast.11, ...), custom_call_target="tpu_custom_call" | custom-call | tf_op jit(solution)/shard_map/pallas_call | solution.py:543
  40.0 1.5 %shard_map.102 = (bf16[256,1024]{1,0:T(8,128)(2,1)}, bf16[256,1024]{1,0:T(8,128)(2,1)}, bf16[256,1024]{1,0:T(8,128)(2,1)}, bf16[256,1024]{1,0:T(8,128)(2,1)}, f32[128,1024]{1,0:T(8,128)}) custom-call(bf16[256,1024]{1,0:T(8,128)(2,1)S(1)} %get-tuple-element.15.refs_0_, bf16[256,1024]{1,0:T(8,128)(2,1)S(1)} %get-tuple-element.16.refs_1_, ...), custom_call_target="tpu_custom_call" | custom-call | tf_op jit(solution)/shard_map/pallas_call | solution.py:597

commit v6 on v5

--- a/solution.py
+++ b/solution.py
@@ -446,10 +446,10 @@
 
     heads_of(3, make_scores)
     last_cut(0)
+    tail_first()
     state_step(1, 0, 3)
     heads_of(2, make_scores)
     last_cut(1)
-    tail_first()
     state_step(1, 0, 2)
     heads_of(1, make_scores)
     last_cut(2)

time: 41.7 us -> 41.7 us (level)
  no operation moved by 1% of the time
where the time goes in v6:
time: 41.7 us; the launch traced here: 41.5 us
  Pallas kernels  40.9 us (98%)
  between operations  0.64 us (2%)
    pallas_call x1, Pallas kernels, on_device(): pl.pallas_call(functools.partial(kernel, n_seq, n_dp), out_shape=[vm((tok...  39.3 us
    pallas_call x1, Pallas kernels, on_device(): pl.pallas_call(store, out_shape=[jax.ShapeDtypeStruct(o.shape, o.dtype) f...  1.53 us

profile of v6, /device:TPU:0, one launch (start us, length us, event | category | flops | bytes accessed | tf_op | source)
XLA Modules:
  0.0 41.5 jit_solution(9406237323916385385)
XLA Ops:
  0.6 39.3 %shard_map.101 = (bf16[256,1024]{1,0:T(8,128)(2,1)S(1)}, bf16[256,1024]{1,0:T(8,128)(2,1)S(1)}, bf16[256,1024]{1,0:T(8,128)(2,1)S(1)}, bf16[256,1024]{1,0:T(8,128)(2,1)S(1)}, f32[128,1024]{1,0:T(8,128)S(1)}) custom-call(bf16[256,1024]{1,0:T(8,128)(2,1)} %bitcast.9, bf16[256,1024]{1,0:T(8,128)(2,1)} %bitcast.10, bf16[256,1024]{1,0:T(8,128)(2,1)} %bitcast.11, ...), custom_call_target="tpu_custom_call" | custom-call | tf_op jit(solution)/shard_map/pallas_call | solution.py:543
  40.0 1.5 %shard_map.102 = (bf16[256,1024]{1,0:T(8,128)(2,1)}, bf16[256,1024]{1,0:T(8,128)(2,1)}, bf16[256,1024]{1,0:T(8,128)(2,1)}, bf16[256,1024]{1,0:T(8,128)(2,1)}, f32[128,1024]{1,0:T(8,128)}) custom-call(bf16[256,1024]{1,0:T(8,128)(2,1)S(1)} %get-tuple-element.15.refs_0_, bf16[256,1024]{1,0:T(8,128)(2,1)S(1)} %get-tuple-element.16.refs_1_, ...), custom_call_target="tpu_custom_call" | custom-call | tf_op jit(solution)/shard_map/pallas_call | solution.py:597
